TPU v7x, 256 devices: a whole 4x4x8 slice. The times are simulated.
256 devices in a mesh: leaf: 8 (over z), wide: 32 (over x, y, core).
Axes of the slice: x: 4, y: 4, z: 8, core: 2. Of those that a mesh axis runs over, the one named last changes fastest.
Arguments:
- points: float32 [64, 1048576], P(None, ('leaf', 'wide')), may hold values from -6 to 6
- leaf_basis: bfloat16 [1048576, 256], P(('leaf', 'wide')), may hold values from -0.25 to 0.25
- right_sides: bfloat16 [32, 1048576], P(None, ('leaf', 'wide')), may hold values from -6 to 6
- leaf_order: int32 [1048576], P(('leaf', 'wide')), may hold values from 0 to 4095, as said below
- local_up: bfloat16 [3584, 256, 256], P(('leaf', 'wide')), may hold values from -0.25 to 0.25
- local_down: bfloat16 [3584, 256, 256], P(('leaf', 'wide')), may hold values from -0.375 to 0.375
- local_links: bfloat16 [1792, 2, 256, 256], P(('leaf', 'wide')), may hold values from -0.109375 to 0.109375
- upper_nodes: bfloat16 [256, 8, 3, 256, 256], P(('leaf', 'wide')), as said below
Outputs:
- kernel_product: float32 [32, 1048576], P(None, ('leaf', 'wide'))
Inputs may be any that keep to these rules, and one draw needn't show every extreme that they name: `leaf_order`: each aligned block of 4096 entries holds every value of 0 to 4095 once. upper_nodes[d, j] is the same for all devices d whose indices (leaf axis the slower) agree after dropping their lowest j bits: the upward matrix, downward matrix and sibling coupling of their common ancestor at height 3 + j.
All inputs are finite; a program needn't handle non-finite values.
Results may differ from a plain program's by a relative error of at most 0.002.
Values sent between devices are 32-bit elements; how exact they have to be, the bound alone decides.
A program may use at most 64 MiB of HBM per device.

v0:
```python
import jax
import jax.numpy as jnp
from jax import lax
from jax.sharding import PartitionSpec as P

HIGHEST = lax.Precision.HIGHEST
RIDGE_TERM = 1.0


def swapped(array, axis, bit):
    return lax.ppermute(array, axis, [(i, i ^ 1 << bit) for i in range(lax.axis_size(axis))])


def kernel_blocks(coords):
    squares = jnp.sum(coords * coords, axis=0)
    inner_prod = jnp.einsum("dal,dam->alm", coords, coords, precision=HIGHEST)
    distance = squares[:, :, None] + squares[:, None, :] - 2.0 * inner_prod
    identity = jnp.eye(coords.shape[2], dtype=jnp.float32)
    blocks = jnp.exp(distance * (-2.0 / coords.shape[0])) + RIDGE_TERM * identity
    return blocks.astype(jnp.bfloat16)


def lifted(values, matrix):
    return jnp.dot(values, matrix.astype(jnp.float32), precision=HIGHEST)


def batched(values, matrices):
    return jnp.einsum("nkr,nrs->nks", values, matrices.astype(jnp.float32), precision=HIGHEST)


def on_device(
    points, leaf_basis, right_sides, leaf_order, local_up, local_down, local_links, upper_nodes
):
    floats = jnp.float32
    dims, pts_dev = points.shape
    rank = leaf_basis.shape[1]
    columns = right_sides.shape[0]
    leaves = local_links.shape[0] + 1
    leaf_size = pts_dev // leaves
    local_levels = leaves.bit_length() - 1
    wide_levels = lax.axis_size("wide").bit_length() - 1
    top_levels = lax.axis_size("leaf").bit_length() - 1
    tree_rhs = jnp.take(right_sides, leaf_order, axis=1).reshape(columns, leaves, leaf_size)
    shaped_basis = leaf_basis.reshape(leaves, leaf_size, rank)
    coefficients = [
        jnp.einsum("kal,alr->akr", tree_rhs, shaped_basis, preferred_element_type=floats)
    ]
    for height in range(1, local_levels + 1):
        number = leaves >> height - 1
        offset = 2 * leaves - 2 * number
        moved = batched(coefficients[-1], local_up[offset : offset + number])
        coefficients.append(moved.reshape(number // 2, 2, columns, rank).sum(axis=1))
    nodes = upper_nodes[0]
    current = coefficients[-1][0]
    siblings = []
    terms = [current]
    for tier in range(wide_levels):
        terms.append(lifted(terms[-1], nodes[tier, 0]))
    every = lax.all_gather(jnp.stack(terms)[None], "wide", axis=0, tiled=True)
    peers = jnp.arange(lax.axis_size("wide"), dtype=jnp.int32)
    position = lax.axis_index("wide")
    for tier in range(wide_levels):
        chosen = (peers >> tier == position >> tier ^ 1).astype(floats)
        siblings.append(jnp.einsum("e,ekr->kr", chosen, every[:, tier], precision=HIGHEST))
    current = jnp.sum(every[:, wide_levels], axis=0)
    for tier in range(top_levels):
        slot = wide_levels + tier
        own_lift = lifted(current, nodes[slot, 0])
        remote, remote_lift = swapped((current, own_lift), "leaf", tier)
        siblings.append(remote)
        current = own_lift + remote_lift
    far_field = jnp.zeros((columns, rank), floats)
    for slot in reversed(range(wide_levels + top_levels)):
        far_field = lifted(far_field, nodes[slot, 1]) + lifted(siblings[slot], nodes[slot, 2])
    far_field = far_field[None]
    for height in reversed(range(local_levels)):
        number = leaves >> height
        offset = 2 * leaves - 2 * number
        first = leaves - number
        sibling = (
            coefficients[height]
            .reshape(number // 2, 2, columns, rank)[:, ::-1]
            .reshape(number, columns, rank)
        )
        couplings = local_links[first : first + number // 2].reshape(number, rank, rank)
        parent = jnp.repeat(far_field, 2, axis=0)
        far_field = batched(parent, local_down[offset : offset + number]) + batched(
            sibling, couplings
        )
    blocks = kernel_blocks(points.reshape(dims, leaves, leaf_size))
    near_part = jnp.einsum("kal,alm->kam", tree_rhs, blocks, preferred_element_type=floats)
    far_part = jnp.einsum(
        "akr,alr->kal", far_field.astype(jnp.bfloat16), shaped_basis, preferred_element_type=floats
    )
    values = (near_part + far_part).reshape(columns, pts_dev)
    return jnp.zeros((columns, pts_dev), floats).at[:, leaf_order].set(values)


def solution(mesh):
    in_specs = (
        P(None, ("leaf", "wide")),
        P(("leaf", "wide"), None),
        P(None, ("leaf", "wide")),
        P(("leaf", "wide")),
        P(("leaf", "wide"), None, None),
        P(("leaf", "wide"), None, None),
        P(("leaf", "wide"), None, None, None),
        P(("leaf", "wide"), None, None, None, None),
    )
    out_specs = P(None, ("leaf", "wide"))
    return jax.shard_map(
        on_device, mesh=mesh, in_specs=in_specs, out_specs=out_specs, check_vma=False
    )
```

profile of v0, /device:TPU:1, one launch (start us, length us, event | category | flops | bytes accessed | tf_op | source)
XLA Modules:
  0.0 154.4 jit_solution(14636876531250342079)
XLA Ops:
  6.5 1.5 broadcast_clamp_fusion
  8.7 1.4 copy.19
  10.2 15.0 %gather_fusion = bf16[4096,32]{1,0:T(8,128)(2,1)} fusion(bf16[32,4096]{0,1:T(8,128)(2,1)S(1)} %copy.19, s32[4096]{0:T(1024)S(1)} %get-tuple-element.11), kind=kCustom, calls=%fused_computation | custom fusion | bytes 540672 | tf_op jit(solution)/shard_map/jit(_take)/gather | solution.py:43
  25.1 1.5 copy.20
  27.4 1.9 %bitcast_reduce_fusion = f32[4,32,256]{2,1,0:T(8,128)S(1)} fusion(f32[8,32,256]{2,1,0:T(8,128)S(1)} %fusion.36, bf16[14,256,256]{2,1,0:T(8,128)(2,1)} %param.12), kind=kOutput, calls=%fused_computation.55 | convolution fusion | flops 201359360 | bytes 1441792 | tf_op jit(solution)/shard_map/nkr,nrs->nks/dot_general | solution.py:28
  29.3 1.5 bitcast_reduce_fusion.1
  31.4 1.8 %bitcast_dynamic-update-slice_fusion.4 = (f32[6,32,256]{2,1,0:T(8,128)}, f32[32,256,1]{1,0,2:T(8,128)S(1)}) fusion(f32[2,32,256]{2,1,0:T(8,128)S(1)} %bitcast_reduce_fusion.1, bf16[14,256,256]{2,1,0:T(8,128)(2,1)} %param.12), kind=kOutput, calls=%fused_computation.113 | convolution fusion | flops 50331648 | bytes 393216 | tf_op jit(solution)/shard_map/nkr,nrs->nks/dot_general | solution.py:28
  33.2 1.7 %bitcast_dynamic-update-slice_fusion.3 = (f32[6,32,256]{2,1,0:T(8,128)}, f32[32,256]{1,0:T(8,128)S(1)}) fusion(f32[6,32,256]{2,1,0:T(8,128)} %get-tuple-element.13, bf16[8,3,256,256]{3,2,1,0:T(8,128)(2,1)} %bitcast.209, f32[32,256,1]{1,0,2:T(8,128)S(1)} %get-tuple-element.14), kind=kOutput, calls=%fused_computation.112 | convolution fusion | flops 25165824 | bytes 229376 | tf_op jit(solution)/shard_map/dot_general | solution.py:24
  34.9 1.7 %bitcast_dynamic-update-slice_fusion.2 = (f32[6,32,256]{2,1,0:T(8,128)}, f32[32,256]{1,0:T(8,128)S(1)}) fusion(f32[6,32,256]{2,1,0:T(8,128)} %get-tuple-element.15, f32[32,256]{1,0:T(8,128)S(1)} %get-tuple-element.16, bf16[8,3,256,256]{3,2,1,0:T(8,128)(2,1)} %bitcast.210), kind=kOutput, calls=%fused_computation.111 | convolution fusion | flops 25165824 | bytes 229376 | tf_op jit(solution)/shard_map/dot_general | solution.py:24
  36.6 1.7 %bitcast_dynamic-update-slice_fusion.1 = (f32[6,32,256]{2,1,0:T(8,128)}, f32[32,256]{1,0:T(8,128)S(1)}) fusion(f32[6,32,256]{2,1,0:T(8,128)} %get-tuple-element.17, f32[32,256]{1,0:T(8,128)S(1)} %get-tuple-element.18, bf16[8,3,256,256]{3,2,1,0:T(8,128)(2,1)} %bitcast.211), kind=kOutput, calls=%fused_computation.110 | convolution fusion | flops 25165824 | bytes 229376 | tf_op jit(solution)/shard_map/dot_general | solution.py:24
  38.3 1.7 %bitcast_dynamic-update-slice_fusion = (f32[6,32,256]{2,1,0:T(8,128)}, f32[32,256]{1,0:T(8,128)S(1)}) fusion(f32[6,32,256]{2,1,0:T(8,128)} %get-tuple-element.19, f32[32,256]{1,0:T(8,128)S(1)} %get-tuple-element.20, bf16[8,3,256,256]{3,2,1,0:T(8,128)(2,1)} %bitcast.212), kind=kOutput, calls=%fused_computation.109 | convolution fusion | flops 25165824 | bytes 229376 | tf_op jit(solution)/shard_map/dot_general | solution.py:24
  40.0 1.7 %fusion.5 = f32[6,32,256]{2,1,0:T(8,128)} fusion(f32[6,32,256]{2,1,0:T(8,128)} %get-tuple-element.21, f32[32,256]{1,0:T(8,128)S(1)} %get-tuple-element.22, bf16[8,3,256,256]{3,2,1,0:T(8,128)(2,1)} %bitcast.213), kind=kOutput, calls=%fused_computation.21 | convolution fusion | flops 25165824 | bytes 196608 | tf_op jit(solution)/shard_map/dot_general | solution.py:24
  41.8 1.5 reshape.84
  46.0 6.7 %fusion.6 = f32[8,512,512]{2,1,0:T(8,128)S(1)} fusion(f32[8,8,8,512]{3,2,1,0:T(8,128)S(1)} %bitcast.206), kind=kOutput, calls=%fused_computation.22 | convolution fusion | flops 1610612736 | bytes 9437184 | tf_op jit(solution)/shard_map/dal,dam->alm/dot_general | solution.py:16
  52.8 2.3 %fusion.1 = f32[32,8,512]{2,0,1:T(8,128)S(1)} fusion(f32[8,512,512]{2,1,0:T(8,128)S(1)} %fusion.6, f32[512,512]{1,0:T(8,128)S(1)} %fusion.25, f32[8,512]{1,0:T(8,128)S(1)} %add.77, bf16[32,8,512]{2,0,1:T(8,128)(2,1)S(1)} %copy-done.6, pred[8,512]{1,0:T(8,128)(4,1)S(1)} %broadcast_in_dim.37), kind=kOutput, calls=%fused_computation.4 | convolution fusion | flops 146931712 | bytes 10244096 | tf_op jit(solution)/shard_map/kal,alm->kam/dot_general | solution.py:91
  55.0 45.3 %all-gather.3.cloned.1.call-done = f32[192,32,256]{2,1,0:T(8,128)} async-done(((f32[6,32,256]{2,1,0:T(8,128)}), f32[192,32,256]{2,1,0:T(8,128)}) %all-gather.3.cloned.1.call-update) | async-done | bytes 6291472 | tf_op jit(solution)/shard_map/all_gather | solution.py:59
  100.3 3.6 %slice_bitcast_fusion = (f32[32,32,256]{2,1,0:T(8,128)S(1)}, f32[32,32,256]{2,1,0:T(8,128)S(1)}, f32[32,32,256]{2,1,0:T(8,128)S(1)}, f32[32,32,256]{2,1,0:T(8,12...) fusion(f32[32,6,32,256]{3,2,1,0:T(8,128)} %bitcast.205), kind=kLoop, calls=%fused_computation.25 | loop fusion | flops 253952 | bytes 11567104 | tf_op jit(solution)/shard_map/squeeze | solution.py:64
  104.3 1.5 collective-permute-start.4
  109.4 2.4 %collective-permute-start.1 = (f32[32,256]{1,0:T(8,128)S(1)}, f32[32,256]{1,0:T(8,128)S(1)}, u32[]{:S(2)}, u32[]{:S(2)}) collective-permute-start(f32[32,256]{1,0:T(8,128)S(1)} %fusion.44), channel_id=1, source_target_pairs={{0,64},{32,96},{64,0},{96,32},{128,192},{160,224},{192,128},{224,1... | collective-permute-start | bytes 98312 | tf_op jit(solution)/shard_map/ppermute | solution.py:11
  113.2 5.8 %collective-permute-start.2 = (f32[32,256]{1,0:T(8,128)S(1)}, f32[32,256]{1,0:T(8,128)S(1)}, u32[]{:S(2)}, u32[]{:S(2)}) collective-permute-start(f32[32,256]{1,0:T(8,128)S(1)} %add.84), channel_id=1, source_target_pairs={{0,128},{32,160},{64,192},{96,224},{128,0},{160,32},{192,64},{224,... | collective-permute-start | bytes 98312 | tf_op jit(solution)/shard_map/ppermute | solution.py:11
  120.8 3.4 %collective-permute-done.3 = f32[32,256]{1,0:T(8,128)S(1)} collective-permute-done((f32[32,256]{1,0:T(8,128)S(1)}, f32[32,256]{1,0:T(8,128)S(1)}, u32[]{:S(2)}, u32[]{:S(2)}) %collective-permute-start.3) | collective-permute-done | bytes 32800 | tf_op jit(solution)/shard_map/ppermute | solution.py:11
  130.3 1.9 %copy.22 = f32[4096,32]{1,0:T(8,128)} copy(f32[4096,32]{0,1:T(8,128)S(1)} %bitcast.233) | data formatting | bytes 1048576 | tf_op jit(solution)/shard_map/reshape | solution.py:95
  132.2 12.3 %scatter_custom_fusion = f32[32,4096]{0,1:T(8,128)} fusion(s32[4096]{0:T(1024)} %get-tuple-element.12, f32[4096,32]{1,0:T(8,128)} %copy.22, f32[]{:T(128)} %constant.12.clone.1), kind=kCustom, calls=%fused_computation.47 | custom fusion | bytes 524800 | tf_op jit(solution)/shard_map/scatter | solution.py:96
  144.6 3.0 %copy.23 = f32[32,4096]{1,0:T(8,128)} copy(f32[32,4096]{0,1:T(8,128)} %scatter_custom_fusion) | data formatting | bytes 1048576 | tf_op jit(solution)/shard_map/scatter | solution.py:96
  (77 shorter events, 17.7 us)
Async XLA Ops:
  6.5 20.2 %copy-start = (bf16[4096,256]{1,0:T(8,128)(2,1)S(1)}, bf16[4096,256]{1,0:T(8,128)(2,1)}, u32[]{:S(2)}) copy-start(bf16[4096,256]{1,0:T(8,128)(2,1)} %param.9) | copy-start | bytes 6291460
  6.5 93.8 %all-gather.3.cloned.1.call-start = ((), (), s32[]{:S(2)}) async-start(), calls=%async_computation | async-start | bytes 6488064 | tf_op jit(solution)/shard_map/all_gather | solution.py:59
  26.7 0.7 copy-start.5
  29.2 15.4 %copy-start.1 = (f32[64,4096]{1,0:T(8,128)S(1)}, f32[64,4096]{1,0:T(8,128)}, u32[]{:S(2)}) copy-start(f32[64,4096]{1,0:T(8,128)} %param.8) | copy-start | bytes 3145732
  30.8 0.6 copy-start.8
  46.0 6.8 %copy-start.6 = (bf16[32,8,512]{2,0,1:T(8,128)(2,1)S(1)}, bf16[32,8,512]{2,0,1:T(8,128)(2,1)}, u32[]{:S(2)}) copy-start(bf16[32,8,512]{2,0,1:T(8,128)(2,1)} %copy-done.5) | copy-start | bytes 786436
  100.3 3.8 %copy-start.3 = (bf16[1,8,3,256,256]{4,3,2,1,0:T(8,128)(2,1)S(1)}, bf16[1,8,3,256,256]{4,3,2,1,0:T(8,128)(2,1)}, u32[]{:S(2)}) copy-start(bf16[1,8,3,256,256]{4,3,2,1,0:T(8,128)(2,1)} %param.15) | copy-start | bytes 9437188
  104.3 20.4 %collective-permute-start.4 = (f32[32,256]{1,0:T(8,128)S(1)}, f32[32,256]{1,0:T(8,128)S(1)}, u32[]{:S(2)}, u32[]{:S(2)}) collective-permute-start(f32[32,256]{1,0:T(8,128)S(1)} %get-tuple-element.10), channel_id=1, source_target_pairs={{0,32},{32,0},{64,96},{96,64},{128,160},{160,128},{192,224},{224,1... | collective-permute-start | bytes 98312 | tf_op jit(solution)/shard_map/ppermute | solution.py:11
  105.8 3.4 %collective-permute-start = (f32[32,256]{1,0:T(8,128)S(1)}, f32[32,256]{1,0:T(8,128)S(1)}, u32[]{:S(2)}, u32[]{:S(2)}) collective-permute-start(f32[32,256]{1,0:T(8,128)S(1)} %fusion.45), channel_id=1, source_target_pairs={{0,32},{32,0},{64,96},{96,64},{128,160},{160,128},{192,224},{224,1... | collective-permute-start | bytes 98312 | tf_op jit(solution)/shard_map/ppermute | solution.py:11
  109.1 17.8 %copy-start.4 = (bf16[14,256,256]{2,1,0:T(8,128)(2,1)S(1)}, bf16[14,256,256]{2,1,0:T(8,128)(2,1)}, u32[]{:S(2)}) copy-start(bf16[14,256,256]{2,1,0:T(8,128)(2,1)} %param.13) | copy-start | bytes 5505028
  109.1 18.0 %copy-start.2 = (bf16[7,2,256,256]{3,2,1,0:T(8,128)(2,1)S(1)}, bf16[7,2,256,256]{3,2,1,0:T(8,128)(2,1)}, u32[]{:S(2)}) copy-start(bf16[7,2,256,256]{3,2,1,0:T(8,128)(2,1)} %param.14) | copy-start | bytes 5505028
  109.2 18.0 %copy-start.10 = (f32[2,32,256]{2,1,0:T(8,128)S(1)}, f32[2,32,256]{2,1,0:T(8,128)}, u32[]{:S(2)}) copy-start(f32[2,32,256]{2,1,0:T(8,128)} %reshape.84) | copy-start | bytes 196612
  109.4 3.8 %collective-permute-start.1 = (f32[32,256]{1,0:T(8,128)S(1)}, f32[32,256]{1,0:T(8,128)S(1)}, u32[]{:S(2)}, u32[]{:S(2)}) collective-permute-start(f32[32,256]{1,0:T(8,128)S(1)} %fusion.44), channel_id=1, source_target_pairs={{0,64},{32,96},{64,0},{96,32},{128,192},{160,224},{192,128},{224,1... | collective-permute-start | bytes 98312 | tf_op jit(solution)/shard_map/ppermute | solution.py:11
  112.8 15.1 %slice-start = ((bf16[7,2,256,256]{3,2,1,0:T(8,128)(2,1)}), bf16[2,2,256,256]{3,2,1,0:T(8,128)(2,1)S(1)}, s32[]{:S(2)}) async-start(bf16[7,2,256,256]{3,2,1,0:T(8,128)(2,1)} %param.14), calls=%async_computation.1 | async-start | bytes 1048576 | tf_op jit(solution)/shard_map/slice | solution.py:85
  112.8 15.1 %copy-start.9 = (f32[2,2,32,256]{3,2,1,0:T(8,128)S(1)}, f32[2,2,32,256]{3,2,1,0:T(8,128)}, u32[]{:S(2)}) copy-start(f32[2,2,32,256]{3,2,1,0:T(8,128)} %rev.7) | copy-start | bytes 393220
  113.2 7.3 %collective-permute-start.2 = (f32[32,256]{1,0:T(8,128)S(1)}, f32[32,256]{1,0:T(8,128)S(1)}, u32[]{:S(2)}, u32[]{:S(2)}) collective-permute-start(f32[32,256]{1,0:T(8,128)S(1)} %add.84), channel_id=1, source_target_pairs={{0,128},{32,160},{64,192},{96,224},{128,0},{160,32},{192,64},{224,... | collective-permute-start | bytes 98312 | tf_op jit(solution)/shard_map/ppermute | solution.py:11
  120.0 4.2 %collective-permute-start.3 = (f32[32,256]{1,0:T(8,128)S(1)}, f32[32,256]{1,0:T(8,128)S(1)}, u32[]{:S(2)}, u32[]{:S(2)}) collective-permute-start(f32[32,256]{1,0:T(8,128)S(1)} %add.83), channel_id=1, source_target_pairs={{0,64},{32,96},{64,0},{96,32},{128,192},{160,224},{192,128},{224,1... | collective-permute-start | bytes 98312 | tf_op jit(solution)/shard_map/ppermute | solution.py:11
  125.5 3.4 %slice-start.1 = ((bf16[7,2,256,256]{3,2,1,0:T(8,128)(2,1)}), bf16[4,2,256,256]{3,2,1,0:T(8,128)(2,1)S(1)}, s32[]{:S(2)}) async-start(bf16[7,2,256,256]{3,2,1,0:T(8,128)(2,1)} %param.14), calls=%async_computation.2 | async-start | bytes 2097152 | tf_op jit(solution)/shard_map/slice | solution.py:85
  125.5 3.4 %copy-start.7 = (f32[4,2,32,256]{3,2,1,0:T(8,128)S(1)}, f32[4,2,32,256]{3,2,1,0:T(8,128)}, u32[]{:S(2)}) copy-start(f32[4,2,32,256]{3,2,1,0:T(8,128)} %rev.8) | copy-start | bytes 786436
Sparse Core Ops, SparseCore 0:
  41.9 58.3 all-gather.2
where the time goes:
time: 156 us; the launch traced here: 154 us
  waiting for transfers between devices  49 us (31%)
  local copies, waits for them, and re-layouts  39.1 us (25%)
  matrix products  36 us (23%)
  between operations  13.9 us (9%)
  starting transfers between devices  10.3 us (7%)
  other arithmetic  6.05 us (4%)
    all_gather x1, waiting for transfers between devices, on_device(): every = lax.all_gather(jnp.stack(terms)[None], 'wide', axis=0, tiled=True)  45.3 us
    gather x2, local copies, waits for them, and re-layouts, on_device(): jnp.take(right_sides, leaf_order, axis=1)  16.5 us
    scatter x2, local copies, waits for them, and re-layouts, on_device(): return jnp.zeros((columns, pts_dev), floats).at[:, leaf_order].set(values)  15.3 us
    dot_general x23, matrix products, lifted(): return jnp.dot(values, matrix.astype(jnp.float32), precision=HIGHEST)  13 us
    ppermute x5, starting transfers between devices, swapped(): lax.ppermute(array, axis, [(i, i ^ 1 << bit) for i in range(lax.axis_size...  10.3 us
    dot_general x9, matrix products, batched(): jnp.einsum('nkr,nrs->nks', values, matrices.astype(jnp.float32), precisio...  7.6 us
    dot_general x1, matrix products, kernel_blocks(): inner_prod = jnp.einsum('dal,dam->alm', coords, coords, precision=HIGHEST)  6.75 us
    dot_general x5, matrix products, on_device(): jnp.einsum('e,ekr->kr', chosen, every[:, tier], precision=HIGHEST)  5.18 us
  transfers between devices with their start and end apart: 6, of which 3 were waited for; matrix products, arithmetic and copies ran while one was open for 13% of the time, Pallas kernels for 0%

commit v1 on v0

v1 whole, which is shorter than its diff:
```python
import math

import jax
import jax.numpy as jnp
from jax import lax
from jax.experimental import pallas as pl
from jax.experimental.pallas import tpu as pltpu
from jax.sharding import PartitionSpec as P

MESH = pl.DeviceIdType.MESH
F32 = jnp.float32
BF16 = jnp.bfloat16
LEAVES = 8
LEAF = 512
RANK = 256
COLS = 32
PTS = 4096
DIMS = 64
LOW = 256
HIGH = PTS // LOW
SCALE = math.sqrt(math.log2(math.e) * 4.0 / DIMS)


def flip(value, mask):
    for bit in (1, 2, 4):
        if mask & bit:
            value = value + bit * (1 - 2 * ((value // bit) % 2))
    return value


def halves(values):
    top = values.astype(BF16)
    rest = (values - top.astype(F32)).astype(BF16)
    return jnp.concatenate([top, rest], axis=0)


def times(values, matrix):
    rows = values.shape[0]
    both = jnp.dot(halves(values), matrix, preferred_element_type=F32)
    return both[:rows] + both[rows:]


def kernel(
    points_h, basis_h, rhs_h, order_h, up_h, down_h, links_h, upper_h,
    out_h,
    points_v, basis_v, rhs_v, order_v, up_v, down_v, links_v, upper_v,
    stack_v, hot_v, x_v, near_v, acc_v, out_v,
    xh0, xh1, xh2, cpl, root_v, sib0, lift1, lift1_in,
    s1_v, l2_v, l3_v, y_in, yq_in, far_v, e_v,
    x_out, x_in, z_out, z_in, y3_v,
    load_sem, store_sem, send_sem, recv_sem,
):
    z = lax.axis_index("leaf")
    w = lax.axis_index("wide")
    c = w % 2
    y = (w // 2) % 4
    x = w // 8

    def device(dz=0, dx=0, dy=0, dc=0):
        return (flip(z, dz), flip(x, dx) * 8 + flip(y, dy) * 2 + flip(c, dc))

    peers = [dict(dc=1)]
    peers += [dict(dy=m) for m in (1, 2, 3)]
    peers += [dict(dy=m, dc=1) for m in (1, 2, 3)]
    peers += [dict(dx=m) for m in (1, 2, 3)]
    peers += [dict(dz=m) for m in range(1, 8)]

    pairs = [
        (order_h, order_v), (rhs_h, rhs_v), (basis_h, basis_v), (up_h, up_v),
        (upper_h, upper_v), (points_h, points_v), (links_h, links_v), (down_h, down_v),
    ]
    loads = [
        pltpu.make_async_copy(src, dst, load_sem.at[i])
        for i, (src, dst) in enumerate(pairs)
    ]
    for load in loads:
        load.start()
    ld_order, ld_rhs, ld_basis, ld_up, ld_upper, ld_points, ld_links, ld_down = loads

    barrier = pltpu.get_barrier_semaphore()
    for peer in peers:
        pl.semaphore_signal(barrier, inc=1, device_id=device(**peer), device_id_type=MESH)

    sends = []

    def send(src, dst, slot, peer):
        copy = pltpu.make_async_remote_copy(
            src_ref=src,
            dst_ref=dst,
            send_sem=send_sem.at[slot],
            recv_sem=recv_sem.at[slot],
            device_id=device(**peer),
            device_id_type=MESH,
        )
        copy.start()
        sends.append(copy)
        return copy

    def order_row(a):
        rows = order_v[pl.ds(a * 4, 4), :]
        return jnp.concatenate([rows[i : i + 1] for i in range(4)], axis=1)

    ld_order.wait()
    ld_rhs.wait()
    for h in range(HIGH):
        stack_v[h * COLS : (h + 1) * COLS, :] = rhs_v[:, h * LOW : (h + 1) * LOW]
    ld_basis.wait()

    def leaf_up(a, carry):
        cols = pl.ds(pl.multiple_of(a * LEAF, LEAF), LEAF)
        row = order_row(a)
        low = row % LOW
        high = row // LOW
        place = lax.broadcasted_iota(jnp.int32, (LOW, LEAF), 0)
        hot = jnp.where(place == low, 1.0, 0.0).astype(BF16)
        hot_v[:, cols] = hot
        every = jnp.dot(stack_v[...], hot, preferred_element_type=F32)
        found = every[:COLS]
        for h in range(1, HIGH):
            found = jnp.where(high == h, every[h * COLS : (h + 1) * COLS], found)
        found = found.astype(BF16)
        x_v[:, cols] = found
        xh0[a] = jnp.dot(found, basis_v[cols, :], preferred_element_type=F32)
        return carry

    lax.fori_loop(0, LEAVES, leaf_up, 0)

    def lift_pair(ref, n, first):
        both = jnp.concatenate([ref[2 * n], ref[2 * n + 1]], axis=1)
        mats = up_v[first + 2 * n : first + 2 * n + 2].reshape(2 * RANK, RANK)
        return times(both, mats)

    ld_up.wait()
    for n in range(4):
        xh1[n] = lift_pair(xh0, n, 0)
    for n in range(2):
        xh2[n] = lift_pair(xh1, n, 8)
    root = lift_pair(xh2, 0, 12)
    root_v[...] = root

    pl.semaphore_wait(barrier, len(peers))
    core = dict(dc=1)
    got_sib0 = send(root_v, sib0, 0, core)
    ld_upper.wait()
    lift = times(root, upper_v[0, 0])
    lift1[0] = lift[:16]
    lift1[1] = lift[16:]
    got_lift1 = send(lift1.at[1 - c], lift1_in, 1, core)

    def near(a, carry):
        cols = pl.ds(pl.multiple_of(a * LEAF, LEAF), LEAF)
        p = points_v[:, cols] * SCALE
        top = p.astype(BF16)
        rest = (p - top.astype(F32)).astype(BF16)
        norm = -0.5 * jnp.sum(p * p, axis=0, keepdims=True)
        n1 = norm.astype(BF16).astype(F32)
        n2 = (norm - n1).astype(BF16).astype(F32)
        n3 = norm - n1 - n2
        row = lax.broadcasted_iota(jnp.int32, (16, LEAF), 0)
        one = jnp.where(row < 6, 1.0, 0.0)
        left = jnp.where(row == 0, n1, jnp.where(row == 1, n2, jnp.where(row == 2, n3, one)))
        right = jnp.where(row == 3, n1, jnp.where(row == 4, n2, jnp.where(row == 5, n3, one)))
        pad = jnp.zeros((48, LEAF), BF16)
        a1 = jnp.concatenate([top, rest, top, left.astype(BF16), pad], axis=0)
        a2 = jnp.concatenate([top, top, rest, right.astype(BF16), pad], axis=0)
        power = lax.dot_general(a1, a2, (((0,), (0,)), ((), ())), preferred_element_type=F32)
        block = jnp.exp2(power).astype(BF16)
        rhs = x_v[:, cols]
        near_v[:, cols] = jnp.dot(rhs, block, preferred_element_type=F32) + rhs.astype(F32)
        return carry

    ld_points.wait()
    lax.fori_loop(0, 2, near, 0)

    got_lift1.wait_recv()
    s1 = lift1[c] + lift1_in[...]
    s1_v[...] = s1

    l2 = times(s1, upper_v[1, 0])
    l3 = times(l2, upper_v[2, 0])
    l2_v[...] = l2
    for q in range(4):
        l3_v[q] = l3[q * 4 : q * 4 + 4]
    got_y = []
    got_yq = []
    for m in (1, 2, 3):
        got_y.append(send(s1_v if m == 1 else l2_v, y_in.at[m - 1], 1 + m, dict(dy=m)))
        got_yq.append(send(l3_v.at[flip(y, m)], yq_in.at[m - 1], 4 + m, dict(dy=m)))

    lax.fori_loop(2, 4, near, 0)

    for copy in got_yq:
        copy.wait_recv()
    s3 = (l3_v[y] + yq_in[0]) + (yq_in[1] + yq_in[2])
    l4 = times(s3, upper_v[3, 0])
    l5 = times(l4, upper_v[4, 0])
    x_out[0, 0] = s3
    x_out[0, 1] = l5
    x_out[1, 0] = l4
    x_out[1, 1] = l5
    got_x = []
    for m in (1, 2, 3):
        got_x.append(send(x_out.at[0 if m == 1 else 1], x_in.at[m - 1], 7 + m, dict(dx=m)))

    for copy in got_y:
        copy.wait_recv()
    e = times(times(y_in[1] + y_in[2], upper_v[2, 2]), upper_v[1, 1])
    e = e + times(y_in[0], upper_v[1, 2])
    e_v[c] = e
    got_e = send(e_v.at[c], e_v.at[c], 11, core)

    lax.fori_loop(4, 6, near, 0)

    for copy in got_x:
        copy.wait_recv()
    s5 = (l5 + x_in[0, 1]) + (x_in[1, 1] + x_in[2, 1])
    l6 = times(s5, upper_v[5, 0])
    l7 = times(l6, upper_v[6, 0])
    z_out[0] = s5
    z_out[1] = l6
    z_out[2] = l7
    got_z = []
    for m in range(1, 8):
        src = z_out.at[m.bit_length() - 1]
        got_z.append(send(src, z_in.at[m - 1], 11 + m, dict(dz=m)))

    c3 = times(x_in[0, 0], upper_v[3, 2])
    c4 = times(x_in[1, 0] + x_in[2, 0], upper_v[4, 2])

    ld_links.wait()
    for m in range(8):
        cpl[m] = times(xh0[m ^ 1], links_v[m // 2, m % 2])
    for m in range(4):
        cpl[8 + m] = times(xh1[m ^ 1], links_v[4 + m // 2, m % 2])
    for m in range(2):
        cpl[12 + m] = times(xh2[m ^ 1], links_v[6, m])
    got_sib0.wait_recv()
    c0 = times(sib0[...], upper_v[0, 2])
    got_e.wait_recv()
    c0 = c0 + times(e_v[...].reshape(COLS, RANK), upper_v[0, 1])

    lax.fori_loop(6, 8, near, 0)

    for copy in got_z:
        copy.wait_recv()
    sib5 = z_in[0]
    sib6 = z_in[1] + z_in[2]
    sib7 = (z_in[3] + z_in[4]) + (z_in[5] + z_in[6])
    c5 = times(sib5, upper_v[5, 2])
    c6 = times(sib6, upper_v[6, 2])
    y7 = times(sib7, upper_v[7, 2])
    y6 = times(y7, upper_v[6, 1]) + c6
    y5 = times(y6, upper_v[5, 1]) + c5
    y4 = times(y5, upper_v[4, 1]) + c4
    y3 = times(y4, upper_v[3, 1]) + c3
    slot = c * 4 + y
    y3_v[slot] = y3
    got_y3 = []
    for i, peer in enumerate(peers[:7]):
        got_y3.append(send(y3_v.at[slot], y3_v.at[slot], 19 + i, peer))
    ld_down.wait()
    for copy in got_y3:
        copy.wait_recv()
    y3 = jnp.concatenate([y3_v[i] for i in range(8)], axis=0)
    y2 = times(y3, upper_v[2, 1])
    y1 = times(y2, upper_v[1, 1])
    current = [times(y1, upper_v[0, 1]) + c0]
    for number, first in ((2, 12), (4, 8), (8, 0)):
        current = [
            times(current[m // 2], down_v[first + m]) + cpl[first + m] for m in range(number)
        ]
    for m in range(8):
        far_v[m] = current[m].astype(BF16)

    acc_v[...] = jnp.zeros_like(acc_v)

    def leaf_out(a, carry):
        cols = pl.ds(pl.multiple_of(a * LEAF, LEAF), LEAF)
        far = lax.dot_general(
            far_v[a], basis_v[cols, :], (((1,), (1,)), ((), ())), preferred_element_type=F32
        )
        total = near_v[:, cols] + far
        high = order_row(a) // LOW
        top = total.astype(BF16)
        rest = (total - top.astype(F32)).astype(BF16)
        tops, rests = [], []
        for h in range(HIGH):
            mask = jnp.where(high == h, 1.0, 0.0).astype(BF16)
            tops.append(top * mask)
            rests.append(rest * mask)
        hot = hot_v[:, cols]
        nt = (((1,), (1,)), ((), ()))
        wide = jnp.concatenate(tops, axis=0)
        slim = jnp.concatenate(rests, axis=0)
        acc_v[...] += lax.dot_general(wide, hot, nt, preferred_element_type=F32) + lax.dot_general(
            slim, hot, nt, preferred_element_type=F32
        )
        return carry

    lax.fori_loop(0, LEAVES, leaf_out, 0)
    for h in range(HIGH):
        out_v[:, h * LOW : (h + 1) * LOW] = acc_v[h * COLS : (h + 1) * COLS, :]
    store = pltpu.make_async_copy(out_v, out_h, store_sem)
    store.start()
    for copy in sends:
        copy.wait_send()
    store.wait()


def on_device(
    points, leaf_basis, right_sides, leaf_order, local_up, local_down, local_links, upper_nodes
):
    vm = pltpu.VMEM
    scratch = [
        vm((DIMS, PTS), F32),
        vm((PTS, RANK), BF16),
        vm((COLS, PTS), BF16),
        vm((32, 128), jnp.int32),
        vm((14, RANK, RANK), BF16),
        vm((14, RANK, RANK), BF16),
        vm((7, 2, RANK, RANK), BF16),
        vm((8, 3, RANK, RANK), BF16),
        vm((HIGH * COLS, LOW), BF16),
        vm((LOW, PTS), BF16),
        vm((COLS, PTS), BF16),
        vm((COLS, PTS), F32),
        vm((HIGH * COLS, LOW), F32),
        vm((COLS, PTS), F32),
        vm((8, COLS, RANK), F32),
        vm((4, COLS, RANK), F32),
        vm((2, COLS, RANK), F32),
        vm((14, COLS, RANK), F32),
        vm((COLS, RANK), F32),
        vm((COLS, RANK), F32),
        vm((2, 16, RANK), F32),
        vm((16, RANK), F32),
        vm((16, RANK), F32),
        vm((16, RANK), F32),
        vm((4, 4, RANK), F32),
        vm((3, 16, RANK), F32),
        vm((3, 4, RANK), F32),
        vm((8, COLS, RANK), BF16),
        vm((2, 16, RANK), F32),
        vm((2, 2, 4, RANK), F32),
        vm((3, 2, 4, RANK), F32),
        vm((3, 4, RANK), F32),
        vm((7, 4, RANK), F32),
        vm((8, 4, RANK), F32),
        pltpu.SemaphoreType.DMA((8,)),
        pltpu.SemaphoreType.DMA,
        pltpu.SemaphoreType.DMA((26,)),
        pltpu.SemaphoreType.DMA((26,)),
    ]
    return pl.pallas_call(
        kernel,
        out_shape=jax.ShapeDtypeStruct((COLS, PTS), F32),
        in_specs=[pl.BlockSpec(memory_space=pl.ANY)] * 8,
        out_specs=pl.BlockSpec(memory_space=pl.ANY),
        scratch_shapes=scratch,
        compiler_params=pltpu.CompilerParams(
            collective_id=0, has_side_effects=True, vmem_limit_bytes=56 * 2**20
        ),
    )(
        points, leaf_basis, right_sides, leaf_order.reshape(32, 128), local_up, local_down,
        local_links, upper_nodes.reshape(8, 3, RANK, RANK),
    )


def solution(mesh):
    in_specs = (
        P(None, ("leaf", "wide")),
        P(("leaf", "wide"), None),
        P(None, ("leaf", "wide")),
        P(("leaf", "wide")),
        P(("leaf", "wide"), None, None),
        P(("leaf", "wide"), None, None),
        P(("leaf", "wide"), None, None, None),
        P(("leaf", "wide"), None, None, None, None),
    )
    out_specs = P(None, ("leaf", "wide"))
    return jax.shard_map(
        on_device, mesh=mesh, in_specs=in_specs, out_specs=out_specs, check_vma=False
    )
```

time: 156 us -> 40.2 us (0.26)
  waiting for transfers between devices: 49 us -> 0 us
  Pallas kernels: 0 us -> 38.1 us
  local copies, waits for them, and re-layouts: 39.1 us -> 1.87 us
  matrix products: 36 us -> 0 us
  between operations: 13.9 us -> 0.01 us
  starting transfers between devices: 10.3 us -> 0 us
  other arithmetic: 6.05 us -> 0 us
    all_gather x1 -> x0, waiting for transfers between devices: 45.3 us -> none  [on_device(): every = lax.all_gather(jnp.stack(terms)[None], 'wide', axis=0, tiled=True)]
    pallas_call x0 -> x1, Pallas kernels: none -> 38.1 us  [on_device(): pl.pallas_call(kernel, out_shape=jax.ShapeDtypeStruct((COLS, PTS), F32),...]
    dot_general x41 -> x0, matrix products: 36 us -> none  [the longest x23 13 us: lifted(): return jnp.dot(values, matrix.astype(jnp.float32), precision=HIGHEST)]
    gather x2 -> x0, local copies, waits for them, and re-layouts: 16.5 us -> none  [on_device(): jnp.take(right_sides, leaf_order, axis=1)]
    scatter x2 -> x0, local copies, waits for them, and re-layouts: 15.3 us -> none  [on_device(): return jnp.zeros((columns, pts_dev), floats).at[:, leaf_order].set(values)]
    ppermute x5 -> x0, starting transfers between devices: 10.3 us -> none  [swapped(): lax.ppermute(array, axis, [(i, i ^ 1 << bit) for i in range(lax.axis_size...]
    ppermute x5 -> x0, waiting for transfers between devices: 3.72 us -> none  [swapped(): lax.ppermute(array, axis, [(i, i ^ 1 << bit) for i in range(lax.axis_size...]
    squeeze x1 -> x0, other arithmetic: 3.64 us -> none  [on_device(): every[:, tier]]
  transfers between devices with their start and end apart: 6 -> 0, of which waited for: 3 -> 0; matrix products, arithmetic and copies ran while one was open for 13% -> 0% of each run, Pallas kernels for 0% -> 0%
where the time goes in v1:
time: 40.2 us; the launch traced here: 40 us
  Pallas kernels  38.1 us (95%)
  local copies, waits for them, and re-layouts  1.87 us (5%)
    pallas_call x1, Pallas kernels, on_device(): pl.pallas_call(kernel, out_shape=jax.ShapeDtypeStruct((COLS, PTS), F32),...  38.1 us
    unnamed x1, local copies, waits for them, and re-layouts  1.87 us

profile of v1, /device:TPU:1, one launch (start us, length us, event | category | flops | bytes accessed | tf_op | source)
XLA Modules:
  0.0 40.0 jit_solution(17189003707014976622)
XLA Ops:
  0.0 38.1 %shard_map.82 = f32[32,4096]{1,0:T(8,128)} custom-call(f32[64,4096]{1,0:T(8,128)} %points_h.1, bf16[4096,256]{1,0:T(8,128)(2,1)} %basis_h.1, bf16[32,4096]{1,0:T(8,128)(2,1)} %rhs_h.1, s32[32,128]{1,0:T(8,128)} %bitcast.3, bf16[14,256,256]{2,1,0:T(8,128)(2,1)} %up_h.1, bf16[14,256,256]{2,1,0:T(8,128)(2,1)} %down_h.1, bf16[7,2,256,256]{3,2,1,0:T(8,128)(2,1)} %links_h.1, ...), custom_call_target="tpu_custom_call" | custom-call | tf_op jit(solution)/shard_map/pallas_call | solution.py:354
  38.1 1.9 %copy.10 = f32[32,4096]{1,0:T(8,128)} copy(f32[32,4096]{1,0:T(8,128)} %shard_map.82) | data formatting | bytes 1048576

commit v2 on v1

v2 whole, which is shorter than its diff:
```python
import math

import jax
import jax.numpy as jnp
from jax import lax
from jax.experimental import pallas as pl
from jax.experimental.pallas import tpu as pltpu
from jax.sharding import PartitionSpec as P

MESH = pl.DeviceIdType.MESH
F32 = jnp.float32
BF16 = jnp.bfloat16
LEAVES = 8
LEAF = 512
RANK = 256
COLS = 32
PTS = 4096
DIMS = 64
LOW = 256
HIGH = PTS // LOW
UP_UNROLL = 1
SCALE = math.sqrt(math.log2(math.e) * 4.0 / DIMS)


def flip(value, mask):
    for bit in (1, 2, 4):
        if mask & bit:
            value = value + bit * (1 - 2 * ((value // bit) % 2))
    return value


def halves(values):
    top = values.astype(BF16)
    rest = (values - top.astype(F32)).astype(BF16)
    return jnp.concatenate([top, rest], axis=0)


def times(values, matrix):
    rows = values.shape[0]
    both = jnp.dot(halves(values), matrix, preferred_element_type=F32)
    return both[:rows] + both[rows:]


def pair(values):
    top = values.astype(BF16)
    return top, (values - top.astype(F32)).astype(BF16)


def times_pair(values, top, rest):
    rows = values.shape[0]
    parts = halves(values)
    both = jnp.dot(parts, top, preferred_element_type=F32)
    return both[:rows] + both[rows:] + jnp.dot(parts[:rows], rest, preferred_element_type=F32)


PLANE = sorted(
    (
        dict(dx=dx, dy=dy, dc=dc)
        for dx in range(4)
        for dy in range(4)
        for dc in range(2)
        if dx or dy or dc
    ),
    key=lambda p: -(p["dx"] > 0) - (p["dx"] == 2) - (p["dy"] > 0) - (p["dy"] == 2),
)
FAR_Z = (4, 3, 5, 2, 6, 7, 1)


def kernel(
    points_h, basis_h, rhs_h, order_h, up_h, down_h, links_h, upper_h,
    out_h,
    points_v, basis_v, rhs_v, order_v, up_v, down_v, links_v, p_v, qb_v,
    stack_v, hot_v, x_v, acc_v, out_v,
    xh0, xh1, xh2, cpl, root_v, sib0, half_v, quart_v, plane_in, low_in, y_in,
    e_v, z_out, z_in, y3_v, m_top, m_rest, w_top, w_rest, w1_v, g_v,
    load_sem, store_sem, one_send, one_recv, plane_send, plane_recv, low_send, low_recv,
):
    z = lax.axis_index("leaf")
    w = lax.axis_index("wide")
    c = w % 2
    y = (w // 2) % 4
    x = w // 8

    def device(dz=0, dx=0, dy=0, dc=0):
        return (flip(z, dz), flip(x, dx) * 8 + flip(y, dy) * 2 + flip(c, dc))

    def quarter(dx=0, dy=0, dc=0):
        return flip(c, dc) * 4 + flip(y, dy)

    def load(i, src, dst):
        copy = pltpu.make_async_copy(src, dst, load_sem.at[i])
        copy.start()
        return copy

    ld_order = load(0, order_h, order_v)
    ld_rhs = load(1, rhs_h, rhs_v)
    ld_basis = load(2, basis_h, basis_v)
    ld_up = load(3, up_h, up_v)
    ld_p = load(4, upper_h.at[:, 0], p_v)

    barrier = pltpu.get_barrier_semaphore()
    peers = PLANE + [dict(dz=m) for m in FAR_Z]
    for peer in peers:
        pl.semaphore_signal(barrier, inc=1, device_id=device(**peer), device_id_type=MESH)

    sends = []

    def send(src, dst, send_sem, recv_sem, peer):
        copy = pltpu.make_async_remote_copy(
            src_ref=src,
            dst_ref=dst,
            send_sem=send_sem,
            recv_sem=recv_sem,
            device_id=device(**peer),
            device_id_type=MESH,
        )
        copy.start()
        return copy

    def send_one(src, dst, slot, peer):
        copy = send(src, dst, one_send.at[slot], one_recv.at[slot], peer)
        sends.append(copy)
        return copy

    def order_row(a):
        rows = order_v[pl.ds(a * 4, 4), :]
        return jnp.concatenate([rows[i : i + 1] for i in range(4)], axis=1)

    def leaf_cols(a):
        return pl.ds(pl.multiple_of(a * LEAF, LEAF), LEAF)

    ld_order.wait()
    ld_rhs.wait()
    for h in range(HIGH):
        stack_v[h * COLS : (h + 1) * COLS, :] = rhs_v[:, h * LOW : (h + 1) * LOW]
    ld_basis.wait()
    ld_points = load(5, points_h, points_v)
    ld_links = load(6, links_h, links_v)
    ld_down = load(7, down_h, down_v)
    ld_qb = load(8, upper_h.at[:, 1:], qb_v)

    def leaf_up(a):
        cols = leaf_cols(a)
        row = order_row(a)
        low = row % LOW
        high = row // LOW
        place = lax.broadcasted_iota(jnp.int32, (LOW, LEAF), 0)
        hot = jnp.where(place == low, 1.0, 0.0).astype(BF16)
        hot_v[:, cols] = hot
        every = jnp.dot(stack_v[...], hot, preferred_element_type=F32)
        found = every[:COLS]
        for h in range(1, HIGH):
            found = jnp.where(high == h, every[h * COLS : (h + 1) * COLS], found)
        found = found.astype(BF16)
        x_v[:, cols] = found
        xh0[a] = jnp.dot(found, basis_v[cols, :], preferred_element_type=F32)

    def leaf_ups(i, carry):
        for j in range(UP_UNROLL):
            leaf_up(i * UP_UNROLL + j)
        return carry

    lax.fori_loop(0, LEAVES // UP_UNROLL, leaf_ups, 0)

    def lift_pair(ref, n, first):
        both = jnp.concatenate([ref[2 * n], ref[2 * n + 1]], axis=1)
        mats = up_v[first + 2 * n : first + 2 * n + 2].reshape(2 * RANK, RANK)
        return times(both, mats)

    ld_up.wait()
    for n in range(4):
        xh1[n] = lift_pair(xh0, n, 0)
    for n in range(2):
        xh2[n] = lift_pair(xh1, n, 8)
    root = lift_pair(xh2, 0, 12)

    ld_p.wait()
    lift = [root]
    for level in range(5):
        lift.append(times(lift[-1], p_v[level]))
    for q in range(8):
        quart_v[2, q] = lift[5][q * 4 : q * 4 + 4]
    pl.semaphore_wait(barrier, len(peers))
    for i, peer in enumerate(PLANE):
        send(quart_v.at[2, quarter(**peer)], plane_in.at[i], plane_send, plane_recv, peer)
    root_v[...] = root
    core = dict(dc=1)
    got_sib0 = send_one(root_v, sib0, 0, core)
    for level in (1, 2):
        for half in range(2):
            half_v[level - 1, half] = lift[level][half * 16 : half * 16 + 16]
    for level in (3, 4):
        for q in range(8):
            quart_v[level - 3, q] = lift[level][q * 4 : q * 4 + 4]

    def scatter(a, parts):
        high = jnp.broadcast_to(order_row(a) // LOW, (16, LEAF))
        rows = []
        for h in range(HIGH):
            mask = jnp.where(high == h, 1.0, 0.0).astype(BF16)
            mask = jnp.concatenate([mask, mask], axis=0)
            rows += [part * mask for part in parts]
        rows = jnp.concatenate(rows, axis=0)
        return lax.dot_general(
            rows, hot_v[:, leaf_cols(a)], (((1,), (1,)), ((), ())), preferred_element_type=F32
        )

    def near(a, carry):
        cols = leaf_cols(a)
        p = points_v[:, cols] * SCALE
        top, rest = pair(p)
        norm = -0.5 * jnp.sum(p * p, axis=0, keepdims=True)
        n1 = norm.astype(BF16).astype(F32)
        n2 = (norm - n1).astype(BF16).astype(F32)
        n3 = norm - n1 - n2
        row = lax.broadcasted_iota(jnp.int32, (16, LEAF), 0)
        one = jnp.where(row < 6, 1.0, 0.0)
        left = jnp.where(row == 0, n1, jnp.where(row == 1, n2, jnp.where(row == 2, n3, one)))
        right = jnp.where(row == 3, n1, jnp.where(row == 4, n2, jnp.where(row == 5, n3, one)))
        pad = jnp.zeros((48, LEAF), BF16)
        a1 = jnp.concatenate([top, rest, top, left.astype(BF16), pad], axis=0)
        a2 = jnp.concatenate([top, top, rest, right.astype(BF16), pad], axis=0)
        power = lax.dot_general(a1, a2, (((0,), (0,)), ((), ())), preferred_element_type=F32)
        block = jnp.exp2(power).astype(BF16)
        rhs = x_v[:, cols]
        total = jnp.dot(rhs, block, preferred_element_type=F32) + rhs.astype(F32)
        both = scatter(a, pair(total))
        for h in range(HIGH):
            at = 2 * h * COLS
            acc_v[h * COLS : (h + 1) * COLS, :] += both[at : at + COLS] + both[at + COLS : at + 2 * COLS]
        return carry

    ld_points.wait()
    acc_v[...] = jnp.zeros_like(acc_v)
    lax.fori_loop(0, 1, near, 0)

    got_y = []
    for i in range(6):
        m = 3 - i // 2
        peer = dict(dy=m, dc=i % 2)
        src = half_v.at[0 if m == 1 else 1, flip(c, i % 2)]
        got_y.append(send_one(src, y_in.at[i], 1 + i, peer))
    lower = [peer for peer in PLANE if peer["dx"]]
    for i, peer in enumerate(lower):
        src = quart_v.at[0 if peer["dx"] == 1 else 1, quarter(**peer)]
        send(src, low_in.at[i], low_send, low_recv, peer)

    lax.fori_loop(1, 6, near, 0)

    pltpu.make_async_copy(plane_in, plane_in, plane_recv).wait()
    s5 = jnp.sum(plane_in[...], axis=0) + quart_v[2, quarter()]
    l6 = times(s5, p_v[5])
    l7 = times(l6, p_v[6])
    z_out[0] = s5
    z_out[1] = l6
    z_out[2] = l7
    got_z = []
    for m in FAR_Z:
        got_z.append(send_one(z_out.at[m.bit_length() - 1], z_in.at[m - 1], 7 + m, dict(dz=m)))

    ld_qb.wait()

    def q_of(level):
        return qb_v[level, 0]

    def b_of(level):
        return qb_v[level, 1]

    m7 = jnp.dot(b_of(7), q_of(6), preferred_element_type=F32)
    both = jnp.dot(
        jnp.concatenate([halves(m7), b_of(6)], axis=0), q_of(5), preferred_element_type=F32
    )
    m7 = both[:RANK] + both[RANK : 2 * RANK]
    m6 = both[2 * RANK :]
    both = jnp.dot(
        jnp.concatenate([halves(m7), halves(m6), b_of(5)], axis=0), q_of(4), preferred_element_type=F32
    )
    m7 = both[:RANK] + both[RANK : 2 * RANK]
    m6 = both[2 * RANK : 3 * RANK] + both[3 * RANK : 4 * RANK]
    m5 = both[4 * RANK :]
    for i, mat in enumerate((m7, m6, m5)):
        mat = times(mat, q_of(3))
        m_top[i * RANK : (i + 1) * RANK], m_rest[i * RANK : (i + 1) * RANK] = pair(mat)

    ld_links.wait()
    for m in range(8):
        cpl[m] = times(xh0[m ^ 1], links_v[m // 2, m % 2])
    for m in range(4):
        cpl[8 + m] = times(xh1[m ^ 1], links_v[4 + m // 2, m % 2])
    for m in range(2):
        cpl[12 + m] = times(xh2[m ^ 1], links_v[6, m])

    for copy in got_y:
        copy.wait_recv()
    sib2 = (y_in[0] + y_in[1]) + (y_in[2] + y_in[3])
    sib1 = y_in[4] + y_in[5]
    e = times(times(sib2, b_of(2)), q_of(1)) + times(sib1, b_of(1))
    e_v[c] = e
    got_e = send_one(e_v.at[c], e_v.at[c], 15, core)

    pltpu.make_async_copy(low_in, low_in, low_recv).wait()
    sib3 = jnp.zeros((4, RANK), F32)
    sib4 = jnp.zeros((4, RANK), F32)
    for i, peer in enumerate(lower):
        if peer["dx"] == 1:
            sib3 = sib3 + low_in[i]
        else:
            sib4 = sib4 + low_in[i]
    c34 = times(times(sib4, b_of(4)), q_of(3)) + times(sib3, b_of(3))

    ld_down.wait()
    t = times(times(jnp.dot(q_of(2), q_of(1), preferred_element_type=F32), q_of(0)), down_v[12])
    w1_v[0] = t
    t = times(times(jnp.dot(q_of(2), q_of(1), preferred_element_type=F32), q_of(0)), down_v[13])
    w1_v[1] = t

    def chain_1(m, carry):
        w1_v[2 + m] = times(w1_v[m // 2], down_v[8 + m])
        return carry

    def chain_0(m, carry):
        top, rest = pair(times(w1_v[2 + m // 2], down_v[m]))
        w_top[m] = top
        w_rest[m] = rest
        return carry

    lax.fori_loop(0, 4, chain_1, 0)
    lax.fori_loop(0, 8, chain_0, 0)

    for copy in got_z:
        copy.wait_recv()
    sib5 = z_in[0]
    sib6 = z_in[1] + z_in[2]
    sib7 = (z_in[3] + z_in[4]) + (z_in[5] + z_in[6])
    y3 = times_pair(jnp.concatenate([sib7, sib6, sib5], axis=1), m_top[...], m_rest[...]) + c34
    mine = quarter()
    y3_v[mine] = y3
    got_y3 = []
    for i, peer in enumerate([p for p in PLANE if p["dx"] == 0]):
        got_y3.append(send_one(y3_v.at[mine], y3_v.at[mine], 16 + i, peer))

    got_sib0.wait_recv()
    got_e.wait_recv()
    current = [times(sib0[...], b_of(0)) + times(e_v[...].reshape(COLS, RANK), q_of(0))]
    for number, first in ((2, 12), (4, 8), (8, 0)):
        current = [
            times(current[m // 2], down_v[first + m]) + cpl[first + m] for m in range(number)
        ]
    for m in range(8):
        g_v[m] = current[m]
    lax.fori_loop(6, 8, near, 0)
    pltpu.make_async_copy(plane_in, plane_in, plane_send).wait()
    pltpu.make_async_copy(low_in, low_in, low_send).wait()
    for copy in sends[:-7]:
        copy.wait_send()

    for copy in got_y3:
        copy.wait_recv()
    y3 = jnp.concatenate([y3_v[i] for i in range(8)], axis=0)

    def leaf_out(a):
        far = (times_pair(y3, w_top[a], w_rest[a]) + g_v[a]).astype(BF16)
        far = lax.dot_general(
            far, basis_v[leaf_cols(a), :], (((1,), (1,)), ((), ())), preferred_element_type=F32
        )
        return scatter(a, (far.astype(BF16),))

    def leaf_outs(i, carry):
        total = leaf_out(2 * i) + leaf_out(2 * i + 1)
        acc_v[...] += total
        return carry

    lax.fori_loop(0, LEAVES // 2, leaf_outs, 0)
    for h in range(HIGH):
        out_v[:, h * LOW : (h + 1) * LOW] = acc_v[h * COLS : (h + 1) * COLS, :]
    store = pltpu.make_async_copy(out_v, out_h, store_sem)
    store.start()
    for copy in sends[-7:]:
        copy.wait_send()
    store.wait()


def on_device(
    points, leaf_basis, right_sides, leaf_order, local_up, local_down, local_links, upper_nodes
):
    vm = pltpu.VMEM
    dma = pltpu.SemaphoreType.DMA
    scratch = [
        vm((DIMS, PTS), F32),
        vm((PTS, RANK), BF16),
        vm((COLS, PTS), BF16),
        vm((32, 128), jnp.int32),
        vm((14, RANK, RANK), BF16),
        vm((14, RANK, RANK), BF16),
        vm((7, 2, RANK, RANK), BF16),
        vm((8, RANK, RANK), BF16),
        vm((8, 2, RANK, RANK), BF16),
        vm((HIGH * COLS, LOW), BF16),
        vm((LOW, PTS), BF16),
        vm((COLS, PTS), BF16),
        vm((HIGH * COLS, LOW), F32),
        vm((COLS, PTS), F32),
        vm((8, COLS, RANK), F32),
        vm((4, COLS, RANK), F32),
        vm((2, COLS, RANK), F32),
        vm((14, COLS, RANK), F32),
        vm((COLS, RANK), F32),
        vm((COLS, RANK), F32),
        vm((2, 2, 16, RANK), F32),
        vm((3, 8, 4, RANK), F32),
        vm((31, 4, RANK), F32),
        vm((24, 4, RANK), F32),
        vm((6, 16, RANK), F32),
        vm((2, 16, RANK), F32),
        vm((3, 4, RANK), F32),
        vm((7, 4, RANK), F32),
        vm((8, 4, RANK), F32),
        vm((3 * RANK, RANK), BF16),
        vm((3 * RANK, RANK), BF16),
        vm((8, RANK, RANK), BF16),
        vm((8, RANK, RANK), BF16),
        vm((6, RANK, RANK), F32),
        vm((8, COLS, RANK), F32),
        dma((9,)),
        dma,
        dma((23,)),
        dma((23,)),
        dma,
        dma,
        dma,
        dma,
    ]
    return pl.pallas_call(
        kernel,
        out_shape=jax.ShapeDtypeStruct((COLS, PTS), F32),
        in_specs=[pl.BlockSpec(memory_space=pl.ANY)] * 8,
        out_specs=pl.BlockSpec(memory_space=pl.ANY),
        scratch_shapes=scratch,
        compiler_params=pltpu.CompilerParams(
            collective_id=0, has_side_effects=True, vmem_limit_bytes=56 * 2**20
        ),
    )(
        points, leaf_basis, right_sides, leaf_order.reshape(32, 128), local_up, local_down,
        local_links, upper_nodes.reshape(8, 3, RANK, RANK),
    )


def solution(mesh):
    in_specs = (
        P(None, ("leaf", "wide")),
        P(("leaf", "wide"), None),
        P(None, ("leaf", "wide")),
        P(("leaf", "wide")),
        P(("leaf", "wide"), None, None),
        P(("leaf", "wide"), None, None),
        P(("leaf", "wide"), None, None, None),
        P(("leaf", "wide"), None, None, None, None),
    )
    out_specs = P(None, ("leaf", "wide"))
    return jax.shard_map(
        on_device, mesh=mesh, in_specs=in_specs, out_specs=out_specs, check_vma=False
    )
```

time: 40.2 us -> 34.6 us (0.86)
  Pallas kernels: 38.1 us -> 32.6 us
    pallas_call x1, Pallas kernels: 38.1 us -> 32.6 us  [on_device(): pl.pallas_call(kernel, out_shape=jax.ShapeDtypeStruct((COLS, PTS), F32),...]
where the time goes in v2:
time: 34.6 us; the launch traced here: 34.4 us
  Pallas kernels  32.6 us (94%)
  local copies, waits for them, and re-layouts  1.87 us (5%)
    pallas_call x1, Pallas kernels, on_device(): pl.pallas_call(kernel, out_shape=jax.ShapeDtypeStruct((COLS, PTS), F32),...  32.6 us
    unnamed x1, local copies, waits for them, and re-layouts  1.87 us

profile of v2, /device:TPU:1, one launch (start us, length us, event | category | flops | bytes accessed | tf_op | source)
XLA Modules:
  0.0 34.4 jit_solution(15381716260143037253)
XLA Ops:
  0.0 32.6 %shard_map.82 = f32[32,4096]{1,0:T(8,128)} custom-call(f32[64,4096]{1,0:T(8,128)} %points_h.1, bf16[4096,256]{1,0:T(8,128)(2,1)} %basis_h.1, bf16[32,4096]{1,0:T(8,128)(2,1)} %rhs_h.1, s32[32,128]{1,0:T(8,128)} %bitcast.3, bf16[14,256,256]{2,1,0:T(8,128)(2,1)} %up_h.1, bf16[14,256,256]{2,1,0:T(8,128)(2,1)} %down_h.1, bf16[7,2,256,256]{3,2,1,0:T(8,128)(2,1)} %links_h.1, ...), custom_call_target="tpu_custom_call" | custom-call | tf_op jit(solution)/shard_map/pallas_call | solution.py:433
  32.6 1.9 %copy.10 = f32[32,4096]{1,0:T(8,128)} copy(f32[32,4096]{1,0:T(8,128)} %shard_map.82) | data formatting | bytes 1048576

commit v3 on v2

--- a/solution.py
+++ b/solution.py
@@ -18,7 +18,6 @@
 DIMS = 64
 LOW = 256
 HIGH = PTS // LOW
-UP_UNROLL = 1
 SCALE = math.sqrt(math.log2(math.e) * 4.0 / DIMS)
 
 
@@ -70,10 +69,10 @@
     points_h, basis_h, rhs_h, order_h, up_h, down_h, links_h, upper_h,
     out_h,
     points_v, basis_v, rhs_v, order_v, up_v, down_v, links_v, p_v, qb_v,
-    stack_v, hot_v, x_v, acc_v, out_v,
+    stack_v, hot_v, mask_v, zs_v, x_v,
     xh0, xh1, xh2, cpl, root_v, sib0, half_v, quart_v, plane_in, low_in, y_in,
     e_v, z_out, z_in, y3_v, m_top, m_rest, w_top, w_rest, w1_v, g_v,
-    load_sem, store_sem, one_send, one_recv, plane_send, plane_recv, low_send, low_recv,
+    load_sem, one_send, one_recv, plane_send, plane_recv, low_send, low_recv,
 ):
     z = lax.axis_index("leaf")
     w = lax.axis_index("wide")
@@ -133,34 +132,33 @@
     ld_rhs.wait()
     for h in range(HIGH):
         stack_v[h * COLS : (h + 1) * COLS, :] = rhs_v[:, h * LOW : (h + 1) * LOW]
+    def gather(a):
+        row = order_row(a)
+        low = row % LOW
+        high = jnp.broadcast_to(row // LOW, (8, LEAF))
+        place = lax.broadcasted_iota(jnp.int32, (LOW, LEAF), 0)
+        hot = jnp.where(place == low, 1.0, 0.0).astype(BF16)
+        every = jnp.dot(stack_v[...], hot, preferred_element_type=F32)
+        every = every.reshape(HIGH, COLS // 8, 8, LEAF)
+        found = every[0]
+        for h in range(1, HIGH):
+            found = jnp.where((high == h)[None], every[h], found)
+        x_v[:, leaf_cols(a)] = found.reshape(COLS, LEAF).astype(BF16)
+
+    def gathers(i, carry):
+        gather(2 * i)
+        gather(2 * i + 1)
+        return carry
+
+    lax.fori_loop(0, LEAVES // 2, gathers, 0)
     ld_basis.wait()
     ld_points = load(5, points_h, points_v)
+    ld_qb = load(8, upper_h.at[:, 1:], qb_v)
     ld_links = load(6, links_h, links_v)
     ld_down = load(7, down_h, down_v)
-    ld_qb = load(8, upper_h.at[:, 1:], qb_v)
-
-    def leaf_up(a):
-        cols = leaf_cols(a)
-        row = order_row(a)
-        low = row % LOW
-        high = row // LOW
-        place = lax.broadcasted_iota(jnp.int32, (LOW, LEAF), 0)
-        hot = jnp.where(place == low, 1.0, 0.0).astype(BF16)
-        hot_v[:, cols] = hot
-        every = jnp.dot(stack_v[...], hot, preferred_element_type=F32)
-        found = every[:COLS]
-        for h in range(1, HIGH):
-            found = jnp.where(high == h, every[h * COLS : (h + 1) * COLS], found)
-        found = found.astype(BF16)
-        x_v[:, cols] = found
-        xh0[a] = jnp.dot(found, basis_v[cols, :], preferred_element_type=F32)
-
-    def leaf_ups(i, carry):
-        for j in range(UP_UNROLL):
-            leaf_up(i * UP_UNROLL + j)
-        return carry
-
-    lax.fori_loop(0, LEAVES // UP_UNROLL, leaf_ups, 0)
+    for a in range(LEAVES):
+        cols = slice(a * LEAF, (a + 1) * LEAF)
+        xh0[a] = jnp.dot(x_v[:, cols], basis_v[cols, :], preferred_element_type=F32)
 
     def lift_pair(ref, n, first):
         both = jnp.concatenate([ref[2 * n], ref[2 * n + 1]], axis=1)
@@ -193,19 +191,15 @@
         for q in range(8):
             quart_v[level - 3, q] = lift[level][q * 4 : q * 4 + 4]
 
-    def scatter(a, parts):
-        high = jnp.broadcast_to(order_row(a) // LOW, (16, LEAF))
+    def spread(a, parts):
         rows = []
         for h in range(HIGH):
-            mask = jnp.where(high == h, 1.0, 0.0).astype(BF16)
+            mask = mask_v[h, :, leaf_cols(a)]
             mask = jnp.concatenate([mask, mask], axis=0)
             rows += [part * mask for part in parts]
-        rows = jnp.concatenate(rows, axis=0)
-        return lax.dot_general(
-            rows, hot_v[:, leaf_cols(a)], (((1,), (1,)), ((), ())), preferred_element_type=F32
-        )
-
-    def near(a, carry):
+        return jnp.concatenate(rows, axis=0)
+
+    def near(a):
         cols = leaf_cols(a)
         p = points_v[:, cols] * SCALE
         top, rest = pair(p)
@@ -224,15 +218,28 @@
         block = jnp.exp2(power).astype(BF16)
         rhs = x_v[:, cols]
         total = jnp.dot(rhs, block, preferred_element_type=F32) + rhs.astype(F32)
-        both = scatter(a, pair(total))
+        high = jnp.broadcast_to(order_row(a) // LOW, (16, LEAF))
+        for h in range(HIGH):
+            mask_v[h, :, cols] = jnp.where(high == h, 1.0, 0.0).astype(BF16)
+        low = jnp.broadcast_to(order_row(a) % LOW, (128, LEAF)).T
+        place = lax.broadcasted_iota(jnp.int32, (LEAF, 128), 1)
+        hot = [jnp.where(low == place + i * 128, 1.0, 0.0).astype(BF16) for i in range(2)]
+        hot = jnp.concatenate(hot, axis=1)
+        hot_v[cols, :] = hot
+        both = jnp.dot(spread(a, pair(total)), hot, preferred_element_type=F32)
         for h in range(HIGH):
             at = 2 * h * COLS
-            acc_v[h * COLS : (h + 1) * COLS, :] += both[at : at + COLS] + both[at + COLS : at + 2 * COLS]
+            piece = both[at : at + COLS] + both[at + COLS : at + 2 * COLS]
+            out_h[:, h * LOW : (h + 1) * LOW] += piece
+
+    def nears(i, carry):
+        near(2 * i)
+        near(2 * i + 1)
         return carry
 
     ld_points.wait()
-    acc_v[...] = jnp.zeros_like(acc_v)
-    lax.fori_loop(0, 1, near, 0)
+    out_h[...] = jnp.zeros_like(out_h)
+    lax.fori_loop(0, 1, nears, 0)
 
     got_y = []
     for i in range(6):
@@ -245,7 +252,7 @@
         src = quart_v.at[0 if peer["dx"] == 1 else 1, quarter(**peer)]
         send(src, low_in.at[i], low_send, low_recv, peer)
 
-    lax.fori_loop(1, 6, near, 0)
+    lax.fori_loop(1, 2, nears, 0)
 
     pltpu.make_async_copy(plane_in, plane_in, plane_recv).wait()
     s5 = jnp.sum(plane_in[...], axis=0) + quart_v[2, quarter()]
@@ -309,23 +316,15 @@
     c34 = times(times(sib4, b_of(4)), q_of(3)) + times(sib3, b_of(3))
 
     ld_down.wait()
-    t = times(times(jnp.dot(q_of(2), q_of(1), preferred_element_type=F32), q_of(0)), down_v[12])
-    w1_v[0] = t
-    t = times(times(jnp.dot(q_of(2), q_of(1), preferred_element_type=F32), q_of(0)), down_v[13])
-    w1_v[1] = t
-
-    def chain_1(m, carry):
+    t = times(jnp.dot(q_of(2), q_of(1), preferred_element_type=F32), q_of(0))
+    for m in range(2):
+        w1_v[m] = times(t, down_v[12 + m])
+
+    for m in range(4):
         w1_v[2 + m] = times(w1_v[m // 2], down_v[8 + m])
-        return carry
-
-    def chain_0(m, carry):
-        top, rest = pair(times(w1_v[2 + m // 2], down_v[m]))
-        w_top[m] = top
-        w_rest[m] = rest
-        return carry
-
-    lax.fori_loop(0, 4, chain_1, 0)
-    lax.fori_loop(0, 8, chain_0, 0)
+    for m in range(8):
+        w_top[m], w_rest[m] = pair(times(w1_v[2 + m // 2], down_v[m]))
+    lax.fori_loop(2, 3, nears, 0)
 
     for copy in got_z:
         copy.wait_recv()
@@ -348,7 +347,7 @@
         ]
     for m in range(8):
         g_v[m] = current[m]
-    lax.fori_loop(6, 8, near, 0)
+    lax.fori_loop(3, 4, nears, 0)
     pltpu.make_async_copy(plane_in, plane_in, plane_send).wait()
     pltpu.make_async_copy(low_in, low_in, low_send).wait()
     for copy in sends[:-7]:
@@ -358,26 +357,28 @@
         copy.wait_recv()
     y3 = jnp.concatenate([y3_v[i] for i in range(8)], axis=0)
 
-    def leaf_out(a):
+    for a in range(LEAVES):
+        cols = slice(a * LEAF, (a + 1) * LEAF)
         far = (times_pair(y3, w_top[a], w_rest[a]) + g_v[a]).astype(BF16)
         far = lax.dot_general(
-            far, basis_v[leaf_cols(a), :], (((1,), (1,)), ((), ())), preferred_element_type=F32
-        )
-        return scatter(a, (far.astype(BF16),))
-
-    def leaf_outs(i, carry):
-        total = leaf_out(2 * i) + leaf_out(2 * i + 1)
-        acc_v[...] += total
+            far, basis_v[cols, :], (((1,), (1,)), ((), ())), preferred_element_type=F32
+        ).astype(BF16)
+        for h in range(HIGH):
+            mask = mask_v[h, :, cols]
+            for i in range(2):
+                at = h * COLS + 16 * i
+                zs_v[at : at + 16, cols] = far[16 * i : 16 * i + 16] * mask
+    def collect(i, carry):
+        rows = pl.ds(pl.multiple_of(i * 256, 256), 256)
+        total = jnp.dot(zs_v[rows, :], hot_v[...], preferred_element_type=F32)
+        for h in range(8):
+            cols = pl.ds(pl.multiple_of((i * 8 + h) * LOW, LOW), LOW)
+            out_h[:, cols] += total[h * COLS : (h + 1) * COLS]
         return carry
 
-    lax.fori_loop(0, LEAVES // 2, leaf_outs, 0)
-    for h in range(HIGH):
-        out_v[:, h * LOW : (h + 1) * LOW] = acc_v[h * COLS : (h + 1) * COLS, :]
-    store = pltpu.make_async_copy(out_v, out_h, store_sem)
-    store.start()
+    lax.fori_loop(0, 2, collect, 0)
     for copy in sends[-7:]:
         copy.wait_send()
-    store.wait()
 
 
 def on_device(
@@ -396,10 +397,10 @@
         vm((8, RANK, RANK), BF16),
         vm((8, 2, RANK, RANK), BF16),
         vm((HIGH * COLS, LOW), BF16),
-        vm((LOW, PTS), BF16),
+        vm((PTS, LOW), BF16),
+        vm((HIGH, 16, PTS), BF16),
+        vm((HIGH * COLS, PTS), BF16),
         vm((COLS, PTS), BF16),
-        vm((HIGH * COLS, LOW), F32),
-        vm((COLS, PTS), F32),
         vm((8, COLS, RANK), F32),
         vm((4, COLS, RANK), F32),
         vm((2, COLS, RANK), F32),
@@ -422,7 +423,6 @@
         vm((6, RANK, RANK), F32),
         vm((8, COLS, RANK), F32),
         dma((9,)),
-        dma,
         dma((23,)),
         dma((23,)),
         dma,
@@ -430,19 +430,23 @@
         dma,
         dma,
     ]
+    operands = [
+        pltpu.with_memory_space_constraint(operand, pltpu.HBM)
+        for operand in (
+            points, leaf_basis, right_sides, leaf_order.reshape(32, 128), local_up, local_down,
+            local_links, upper_nodes.reshape(8, 3, RANK, RANK),
+        )
+    ]
     return pl.pallas_call(
         kernel,
-        out_shape=jax.ShapeDtypeStruct((COLS, PTS), F32),
-        in_specs=[pl.BlockSpec(memory_space=pl.ANY)] * 8,
-        out_specs=pl.BlockSpec(memory_space=pl.ANY),
+        out_shape=pltpu.VMEM((COLS, PTS), F32),
+        in_specs=[pl.BlockSpec(memory_space=pltpu.HBM)] * 8,
+        out_specs=pl.BlockSpec(memory_space=pltpu.VMEM),
         scratch_shapes=scratch,
         compiler_params=pltpu.CompilerParams(
-            collective_id=0, has_side_effects=True, vmem_limit_bytes=56 * 2**20
+            collective_id=0, has_side_effects=True, vmem_limit_bytes=48 * 2**20
         ),
-    )(
-        points, leaf_basis, right_sides, leaf_order.reshape(32, 128), local_up, local_down,
-        local_links, upper_nodes.reshape(8, 3, RANK, RANK),
-    )
+    )(*operands)
 
 
 def solution(mesh):

time: 34.6 us -> 30.7 us (0.89)
  Pallas kernels: 32.6 us -> 29.8 us
  local copies, waits for them, and re-layouts: 1.87 us -> 0.8 us
    pallas_call x1, Pallas kernels: 32.6 us -> 29.8 us  [on_device(): pl.pallas_call(kernel, out_shape=pltpu.VMEM((COLS, PTS), F32), in_specs=[...]
    unnamed x1, local copies, waits for them, and re-layouts: 1.87 us -> 0.8 us
where the time goes in v3:
time: 30.7 us; the launch traced here: 30.6 us
  Pallas kernels  29.8 us (97%)
  local copies, waits for them, and re-layouts  0.8 us (3%)
    pallas_call x1, Pallas kernels, on_device(): pl.pallas_call(kernel, out_shape=pltpu.VMEM((COLS, PTS), F32), in_specs=[...  29.8 us
    unnamed x1, local copies, waits for them, and re-layouts  0.8 us

profile of v3, /device:TPU:1, one launch (start us, length us, event | category | flops | bytes accessed | tf_op | source)
XLA Modules:
  0.0 30.6 jit_solution(15608755465819872378)
XLA Ops:
  0.0 29.8 %shard_map.82 = f32[32,4096]{1,0:T(8,128)S(1)} custom-call(f32[64,4096]{1,0:T(8,128)} %points_h.1, bf16[4096,256]{1,0:T(8,128)(2,1)} %basis_h.1, bf16[32,4096]{1,0:T(8,128)(2,1)} %rhs_h.1, s32[32,128]{1,0:T(8,128)} %bitcast.3, bf16[14,256,256]{2,1,0:T(8,128)(2,1)} %up_h.1, bf16[14,256,256]{2,1,0:T(8,128)(2,1)} %down_h.1, bf16[7,2,256,256]{3,2,1,0:T(8,128)(2,1)} %links_h.1, ...), custom_call_target="tpu_custom_call" | custom-call | tf_op jit(solution)/shard_map/pallas_call | solution.py:440
  29.8 0.8 %copy.10 = f32[32,4096]{1,0:T(8,128)} copy(f32[32,4096]{1,0:T(8,128)S(1)} %shard_map.82) | data formatting | bytes 1048576

commit v4 on v3

--- a/solution.py
+++ b/solution.py
@@ -80,11 +80,18 @@
     y = (w // 2) % 4
     x = w // 8
 
+    zs = [flip(z, m) for m in range(8)]
+    xs = [flip(x, m) * 8 for m in range(4)]
+    ys = [flip(y, m) for m in range(4)]
+    cs = [c, 1 - c]
+    yc = [[ys[m] * 2 + cs[i] for i in range(2)] for m in range(4)]
+    quarters = [[cs[i] * 4 + ys[m] for i in range(2)] for m in range(4)]
+
     def device(dz=0, dx=0, dy=0, dc=0):
-        return (flip(z, dz), flip(x, dx) * 8 + flip(y, dy) * 2 + flip(c, dc))
+        return (zs[dz], xs[dx] + yc[dy][dc])
 
     def quarter(dx=0, dy=0, dc=0):
-        return flip(c, dc) * 4 + flip(y, dy)
+        return quarters[dy][dc]
 
     def load(i, src, dst):
         copy = pltpu.make_async_copy(src, dst, load_sem.at[i])
@@ -146,16 +153,20 @@
         x_v[:, leaf_cols(a)] = found.reshape(COLS, LEAF).astype(BF16)
 
     def gathers(i, carry):
-        gather(2 * i)
-        gather(2 * i + 1)
+        for j in range(4):
+            gather(4 * i + j)
         return carry
 
-    lax.fori_loop(0, LEAVES // 2, gathers, 0)
+    lax.fori_loop(0, LEAVES // 4, gathers, 0)
     ld_basis.wait()
+    ld_up.wait()
+    ld_p.wait()
     ld_points = load(5, points_h, points_v)
     ld_qb = load(8, upper_h.at[:, 1:], qb_v)
     ld_links = load(6, links_h, links_v)
     ld_down = load(7, down_h, down_v)
+    p01 = jnp.dot(p_v[0], p_v[1], preferred_element_type=F32)
+    p23 = jnp.dot(p_v[2], p_v[3], preferred_element_type=F32)
     for a in range(LEAVES):
         cols = slice(a * LEAF, (a + 1) * LEAF)
         xh0[a] = jnp.dot(x_v[:, cols], basis_v[cols, :], preferred_element_type=F32)
@@ -165,23 +176,23 @@
         mats = up_v[first + 2 * n : first + 2 * n + 2].reshape(2 * RANK, RANK)
         return times(both, mats)
 
-    ld_up.wait()
     for n in range(4):
         xh1[n] = lift_pair(xh0, n, 0)
+    p03 = times_pair(p01, *pair(p23))
     for n in range(2):
         xh2[n] = lift_pair(xh1, n, 8)
+    p04 = pair(times(p03, p_v[4]))
     root = lift_pair(xh2, 0, 12)
-
-    ld_p.wait()
-    lift = [root]
-    for level in range(5):
-        lift.append(times(lift[-1], p_v[level]))
+    lift5 = times_pair(root, *p04)
     for q in range(8):
-        quart_v[2, q] = lift[5][q * 4 : q * 4 + 4]
+        quart_v[2, q] = lift5[q * 4 : q * 4 + 4]
     pl.semaphore_wait(barrier, len(peers))
     for i, peer in enumerate(PLANE):
         send(quart_v.at[2, quarter(**peer)], plane_in.at[i], plane_send, plane_recv, peer)
     root_v[...] = root
+    lift = [root]
+    for level in range(4):
+        lift.append(times(lift[-1], p_v[level]))
     core = dict(dc=1)
     got_sib0 = send_one(root_v, sib0, 0, core)
     for level in (1, 2):
@@ -245,7 +256,7 @@
     for i in range(6):
         m = 3 - i // 2
         peer = dict(dy=m, dc=i % 2)
-        src = half_v.at[0 if m == 1 else 1, flip(c, i % 2)]
+        src = half_v.at[0 if m == 1 else 1, cs[i % 2]]
         got_y.append(send_one(src, y_in.at[i], 1 + i, peer))
     lower = [peer for peer in PLANE if peer["dx"]]
     for i, peer in enumerate(lower):
@@ -254,10 +265,11 @@
 
     lax.fori_loop(1, 2, nears, 0)
 
+    p56 = pair(jnp.dot(p_v[5], p_v[6], preferred_element_type=F32))
     pltpu.make_async_copy(plane_in, plane_in, plane_recv).wait()
     s5 = jnp.sum(plane_in[...], axis=0) + quart_v[2, quarter()]
     l6 = times(s5, p_v[5])
-    l7 = times(l6, p_v[6])
+    l7 = times_pair(s5, *p56)
     z_out[0] = s5
     z_out[1] = l6
     z_out[2] = l7
@@ -369,14 +381,14 @@
                 at = h * COLS + 16 * i
                 zs_v[at : at + 16, cols] = far[16 * i : 16 * i + 16] * mask
     def collect(i, carry):
-        rows = pl.ds(pl.multiple_of(i * 256, 256), 256)
+        rows = pl.ds(pl.multiple_of(i * 512, 512), 512)
         total = jnp.dot(zs_v[rows, :], hot_v[...], preferred_element_type=F32)
-        for h in range(8):
-            cols = pl.ds(pl.multiple_of((i * 8 + h) * LOW, LOW), LOW)
+        for h in range(HIGH):
+            cols = pl.ds(pl.multiple_of((i * HIGH + h) * LOW, LOW), LOW)
             out_h[:, cols] += total[h * COLS : (h + 1) * COLS]
         return carry
 
-    lax.fori_loop(0, 2, collect, 0)
+    lax.fori_loop(0, 1 + w // 32, collect, 0)
     for copy in sends[-7:]:
         copy.wait_send()
 

time: 30.7 us -> 29.2 us (0.951)
  Pallas kernels: 29.8 us -> 28.3 us
    pallas_call x1, Pallas kernels: 29.8 us -> 28.3 us  [on_device(): pl.pallas_call(kernel, out_shape=pltpu.VMEM((COLS, PTS), F32), in_specs=[...]
where the time goes in v4:
time: 29.2 us; the launch traced here: 29.1 us
  Pallas kernels  28.3 us (97%)
  local copies, waits for them, and re-layouts  0.8 us (3%)
    pallas_call x1, Pallas kernels, on_device(): pl.pallas_call(kernel, out_shape=pltpu.VMEM((COLS, PTS), F32), in_specs=[...  28.3 us
    unnamed x1, local copies, waits for them, and re-layouts  0.8 us

profile of v4, /device:TPU:1, one launch (start us, length us, event | category | flops | bytes accessed | tf_op | source)
XLA Modules:
  0.0 29.1 jit_solution(10667105597670863451)
XLA Ops:
  0.0 28.3 %shard_map.82 = f32[32,4096]{1,0:T(8,128)S(1)} custom-call(f32[64,4096]{1,0:T(8,128)} %points_h.1, bf16[4096,256]{1,0:T(8,128)(2,1)} %basis_h.1, bf16[32,4096]{1,0:T(8,128)(2,1)} %rhs_h.1, s32[32,128]{1,0:T(8,128)} %bitcast.3, bf16[14,256,256]{2,1,0:T(8,128)(2,1)} %up_h.1, bf16[14,256,256]{2,1,0:T(8,128)(2,1)} %down_h.1, bf16[7,2,256,256]{3,2,1,0:T(8,128)(2,1)} %links_h.1, ...), custom_call_target="tpu_custom_call" | custom-call | tf_op jit(solution)/shard_map/pallas_call | solution.py:452
  28.3 0.8 %copy.10 = f32[32,4096]{1,0:T(8,128)} copy(f32[32,4096]{1,0:T(8,128)S(1)} %shard_map.82) | data formatting | bytes 1048576

commit v5 on v4

--- a/solution.py
+++ b/solution.py
@@ -264,6 +264,7 @@
         send(src, low_in.at[i], low_send, low_recv, peer)
 
     lax.fori_loop(1, 2, nears, 0)
+    near(4)
 
     p56 = pair(jnp.dot(p_v[5], p_v[6], preferred_element_type=F32))
     pltpu.make_async_copy(plane_in, plane_in, plane_recv).wait()
@@ -309,6 +310,15 @@
     for m in range(2):
         cpl[12 + m] = times(xh2[m ^ 1], links_v[6, m])
 
+    ld_down.wait()
+    t = times(jnp.dot(q_of(2), q_of(1), preferred_element_type=F32), q_of(0))
+    for m in range(2):
+        w1_v[m] = times(t, down_v[12 + m])
+
+    for m in range(4):
+        w1_v[2 + m] = times(w1_v[m // 2], down_v[8 + m])
+    for m in range(8):
+        w_top[m], w_rest[m] = pair(times(w1_v[2 + m // 2], down_v[m]))
     for copy in got_y:
         copy.wait_recv()
     sib2 = (y_in[0] + y_in[1]) + (y_in[2] + y_in[3])
@@ -327,16 +337,6 @@
             sib4 = sib4 + low_in[i]
     c34 = times(times(sib4, b_of(4)), q_of(3)) + times(sib3, b_of(3))
 
-    ld_down.wait()
-    t = times(jnp.dot(q_of(2), q_of(1), preferred_element_type=F32), q_of(0))
-    for m in range(2):
-        w1_v[m] = times(t, down_v[12 + m])
-
-    for m in range(4):
-        w1_v[2 + m] = times(w1_v[m // 2], down_v[8 + m])
-    for m in range(8):
-        w_top[m], w_rest[m] = pair(times(w1_v[2 + m // 2], down_v[m]))
-    lax.fori_loop(2, 3, nears, 0)
 
     for copy in got_z:
         copy.wait_recv()
@@ -360,6 +360,7 @@
     for m in range(8):
         g_v[m] = current[m]
     lax.fori_loop(3, 4, nears, 0)
+    near(5)
     pltpu.make_async_copy(plane_in, plane_in, plane_send).wait()
     pltpu.make_async_copy(low_in, low_in, low_send).wait()
     for copy in sends[:-7]:

time: 29.2 us -> 29.1 us (level)
  no operation moved by 1% of the time
where the time goes in v5:
time: 29.1 us; the launch traced here: 29 us
  Pallas kernels  28.2 us (97%)
  local copies, waits for them, and re-layouts  0.8 us (3%)
    pallas_call x1, Pallas kernels, on_device(): pl.pallas_call(kernel, out_shape=pltpu.VMEM((COLS, PTS), F32), in_specs=[...  28.2 us
    unnamed x1, local copies, waits for them, and re-layouts  0.8 us

profile of v5, /device:TPU:1, one launch (start us, length us, event | category | flops | bytes accessed | tf_op | source)
XLA Modules:
  0.0 29.0 jit_solution(3705612457617544942)
XLA Ops:
  0.0 28.2 %shard_map.82 = f32[32,4096]{1,0:T(8,128)S(1)} custom-call(f32[64,4096]{1,0:T(8,128)} %points_h.1, bf16[4096,256]{1,0:T(8,128)(2,1)} %basis_h.1, bf16[32,4096]{1,0:T(8,128)(2,1)} %rhs_h.1, s32[32,128]{1,0:T(8,128)} %bitcast.3, bf16[14,256,256]{2,1,0:T(8,128)(2,1)} %up_h.1, bf16[14,256,256]{2,1,0:T(8,128)(2,1)} %down_h.1, bf16[7,2,256,256]{3,2,1,0:T(8,128)(2,1)} %links_h.1, ...), custom_call_target="tpu_custom_call" | custom-call | tf_op jit(solution)/shard_map/pallas_call | solution.py:453
  28.2 0.8 %copy.10 = f32[32,4096]{1,0:T(8,128)} copy(f32[32,4096]{1,0:T(8,128)S(1)} %shard_map.82) | data formatting | bytes 1048576
